TPU v7x, 256 devices: a whole 4x4x8 slice. The times are simulated.
256 devices in a mesh: rep: 4 (over y), fsdp: 16 (over z, x_hi), tp: 4 (over x_lo, core).
Axes of the slice: x: 4 (x_hi: 2, x_lo: 2; x = x_hi * 2 + x_lo), y: 4, z: 8, core: 2. Of those that a mesh axis runs over, the one named last changes fastest.
Arguments:
- grad_parts: bfloat16 [4, 32, 4096, 1536], P('rep', None, 'fsdp', 'tp'), may hold values from -3 to 3
- momentum: bfloat16 [32, 4096, 1536], P('rep', 'fsdp', 'tp'), may hold values from -40 to 40
- basis: bfloat16 [32, 1536, 256], P('rep', 'tp'), may hold values from -0.15625 to 0.15625
Outputs:
- momentum_next: bfloat16 [32, 4096, 1536], P('rep', 'fsdp', 'tp')
- basis_next: bfloat16 [32, 1536, 256], P('rep', 'tp')
- update: bfloat16 [32, 4096, 1536], P('rep', 'fsdp', 'tp')
All inputs are finite; a program needn't handle non-finite values.
Results may differ from a plain program's by a relative error of at most 0.023.
Values may be sent and summed in bfloat16 or wider, within the bound.
A program may use at most 64 MiB of HBM per device.

v0:
```python
import jax
import jax.numpy as jnp
from jax import lax
from jax.sharding import PartitionSpec as P

D = 4096
FF = 1536
RANK = 256


def orthonormal(power, gramian):
    factor = jnp.linalg.cholesky(gramian)
    solved = lax.linalg.triangular_solve(
        factor, power, left_side=False, lower=True, transpose_a=True
    )
    return solved.astype(jnp.bfloat16)


def on_device(grad_parts, momentum, basis):
    local_parts = grad_parts[0]
    gradient = lax.psum_scatter(local_parts, "rep", scatter_dimension=0, tiled=True).astype(
        jnp.float32
    )
    buffer = momentum.astype(jnp.float32) + gradient
    buffer_bf = buffer.astype(jnp.bfloat16)
    partial_power = jnp.einsum("emn,enr->emr", buffer_bf, basis, preferred_element_type=jnp.float32)
    power = lax.psum(partial_power, "tp")
    local_gram = jnp.einsum("emr,ems->ers", power, power, precision=lax.Precision.HIGHEST)
    gramian = lax.psum(local_gram, "fsdp")
    ortho_bf = orthonormal(power, gramian)
    right_part = jnp.einsum("emn,emr->enr", buffer_bf, ortho_bf, preferred_element_type=jnp.float32)
    right_full = lax.psum(right_part, "fsdp")
    squares = lax.psum(jnp.sum(right_full * right_full, axis=1), "tp")
    basis_next = (right_full * lax.rsqrt(squares + 1e-06)[:, None, :]).astype(jnp.bfloat16)
    right_bf = right_full.astype(jnp.bfloat16)
    feedback = jnp.einsum("emr,enr->emn", ortho_bf, right_bf, preferred_element_type=jnp.float32)
    momentum_next = (buffer - 0.05 * feedback).astype(jnp.bfloat16)
    scale_factor = (D * FF / RANK) ** 0.5
    update = (
        scale_factor
        * jnp.einsum("emr,enr->emn", ortho_bf, basis_next, preferred_element_type=jnp.float32)
    ).astype(jnp.bfloat16)
    return (momentum_next, basis_next, update)


def solution(mesh):
    placed = (P("rep", None, "fsdp", "tp"), P("rep", "fsdp", "tp"), P("rep", "tp", None))
    return jax.shard_map(
        on_device,
        mesh=mesh,
        in_specs=placed,
        out_specs=(P("rep", "fsdp", "tp"), P("rep", "tp", None), P("rep", "fsdp", "tp")),
        check_vma=False,
    )
```

profile of v0, /device:TPU:1, one launch (start us, length us, event | category | flops | bytes accessed | tf_op | source)
XLA Modules:
  0.0 990.7 jit_solution(16821015647929866738)
XLA Ops:
  7.2 0.0 copy-start
  7.2 0.0 reduce-scatter.2.cloned.1.call-start
  7.2 0.0 copy-start.3
  7.2 0.7 reduce-scatter.2.cloned.1.call-update
  7.9 0.0 all-reduce.5.cloned.1.call-start
  8.0 73.0 %reduce-scatter.2.cloned.1.call-done = bf16[8,256,384]{2,1,0:T(8,128)(2,1)} async-done(((bf16[32,256,384]{2,1,0:T(8,128)(2,1)}), bf16[8,256,384]{2,1,0:T(8,128)(2,1)}) %reduce-scatter.2.cloned.1.call-update) | async-done | bytes 1572880 | tf_op jit(solution)/shard_map/reduce_scatter | solution.py:21
  81.0 0.0 copy-done
  81.0 0.0 copy-done.3
  81.0 3.4 fusion.7
  84.4 0.0 all-reduce.5.cloned.1.call-update
  84.4 0.0 all-reduce.7.cloned.1.call-start
  84.5 62.6 %all-reduce.5.cloned.1.call-done = f32[8,256,256]{2,1,0:T(8,128)} async-done(((f32[8,256,256]{2,1,0:T(8,128)}), f32[8,256,256]{2,1,0:T(8,128)}) %all-reduce.5.cloned.1.call-update) | async-done | bytes 2097168 | tf_op jit(solution)/shard_map/psum | solution.py:27
  147.1 7.0 fusion.18
  154.2 0.0 all-reduce.7.cloned.1.call-update
  154.2 0.2 all-reduce.9.cloned.1.call-start
  154.5 157.4 %all-reduce.7.cloned.1.call-done = f32[8,256,256]{1,2,0:T(8,128)} async-done(((f32[8,256,256]{1,2,0:T(8,128)}), f32[8,256,256]{1,2,0:T(8,128)}) %all-reduce.7.cloned.1.call-update) | async-done | bytes 2097168 | tf_op jit(solution)/shard_map/psum | solution.py:29
  311.9 2.9 copy.20
  314.8 2.5 fusion.1
  317.4 0.0 copy-start.6
  317.4 1.3 copy-done.6
  318.7 0.8 cholesky.122
  319.5 95.2 %custom-call.16 = f32[8,128,128]{2,1,0:T(8,128)} custom-call(f32[8,128,128]{2,1,0:T(8,128)} %cholesky.122), custom_call_target="Cholesky" | custom-call | tf_op jit(solution)/shard_map/jit(cholesky)/cholesky | solution.py:12
  414.8 2.6 cholesky.117
  417.4 0.0 copy-done.11
  417.4 0.8 select_bitcast_fusion
  418.2 80.0 %custom-call.17 = f32[8,1,128,128]{2,3,1,0:T(8,128)} custom-call(f32[8,1,128,128]{3,2,1,0:T(8,128)} %select_bitcast_fusion), custom_call_target="InvertDiagBlocksLowerTriangular" | custom-call | tf_op jit(solution)/shard_map/jit(cholesky)/cholesky | solution.py:12
  498.2 2.7 constant_dynamic-update-slice_fusion.1
  500.9 3.1 convolution_subtract_fusion.1
  504.0 95.2 %custom-call.18 = f32[8,128,128]{2,1,0:T(8,128)} custom-call(f32[8,128,128]{2,1,0:T(8,128)} %convolution_subtract_fusion.1), custom_call_target="Cholesky" | custom-call | tf_op jit(solution)/shard_map/jit(cholesky)/cholesky | solution.py:12
  599.2 2.1 select_reduce_fusion
  601.3 0.1 compare_reduce_fusion
  601.5 3.2 select_select_fusion
  604.7 0.1 triangular_solve.63
  604.8 8.1 while.1
  604.8 0.6 fusion.28
  605.4 3.6 bitcast_dynamic-update-slice_fusion.2
  608.9 0.6 fusion.28
  609.5 3.4 bitcast_dynamic-update-slice_fusion.2
  612.9 158.6 %custom-call.19 = f32[8,2,128,128]{2,3,1,0:T(8,128)} custom-call(f32[8,2,128,128]{3,2,1,0:T(8,128)} %bitcast.44), custom_call_target="InvertDiagBlocksLowerTriangular" | custom-call | tf_op jit(solution)/shard_map/triangular_solve | solution.py:13
  771.5 2.6 fusion.17
  774.1 0.0 copy-start.7
  774.1 0.0 copy-start.13
  774.1 0.0 copy-done.2
  774.1 0.0 copy-start.4
  774.2 3.2 convolution_subtract_fusion
  777.4 0.0 copy-done.13
  777.4 1.1 convolution_convert_fusion
  778.5 0.0 copy-start.9
  778.5 0.0 copy-done.7
  778.5 0.8 copy-done.9
  779.3 0.0 copy-done.4
  779.3 2.4 fusion.5
  781.7 0.0 all-reduce.9.cloned.1.call-update
  781.7 178.6 %all-reduce.9.cloned.1.call-done = f32[8,384,256]{2,1,0:T(8,128)} async-done(((f32[8,384,256]{2,1,0:T(8,128)}), f32[8,384,256]{2,1,0:T(8,128)}) %all-reduce.9.cloned.1.call-update) | async-done | bytes 3145744 | tf_op jit(solution)/shard_map/psum | solution.py:32
  960.3 2.1 multiply_reduce_fusion
  962.4 13.9 %psum.31 = f32[8,256]{1,0:T(8,128)S(1)} all-reduce(f32[8,256]{1,0:T(8,128)S(1)} %multiply_reduce_fusion), channel_id=1, replica_groups=mesh['rep'=4,'fsdp'=16,'tp'=4] {'tp'}, use_global_device_ids=true, to_apply=%region_9.10 | all-reduce | flops 2048 | bytes 16384 | tf_op jit(solution)/shard_map/psum | solution.py:33
  976.4 0.0 copy-start.8
  976.4 0.0 copy-start.10
  976.4 2.3 multiply_convert_fusion.1
  978.8 0.0 copy-start.12
  978.8 2.0 multiply_convert_fusion
  980.8 0.0 copy-done.5
  980.8 1.1 copy-done.1
  981.9 2.3 subtract_convert_fusion
  (16 shorter events, 0.1 us)
Async XLA Ops:
  7.2 73.8 %copy-start = (bf16[8,384,256]{2,1,0:T(8,128)(2,1)S(1)}, bf16[8,384,256]{2,1,0:T(8,128)(2,1)}, u32[]{:S(2)}) copy-start(bf16[8,384,256]{2,1,0:T(8,128)(2,1)} %param.5) | copy-start | bytes 4718596
  7.2 73.8 %reduce-scatter.2.cloned.1.call-start = ((), (), s32[]{:S(2)}) async-start(), calls=%async_computation.1 | async-start | bytes 7864320 | tf_op jit(solution)/shard_map/reduce_scatter | solution.py:21
  7.2 73.8 %copy-start.3 = (bf16[8,256,384]{2,1,0:T(8,128)(2,1)S(1)}, bf16[8,256,384]{2,1,0:T(8,128)(2,1)}, u32[]{:S(2)}) copy-start(bf16[8,256,384]{2,1,0:T(8,128)(2,1)} %param.4) | copy-start | bytes 4718596
  7.9 139.2 %all-reduce.5.cloned.1.call-start = ((), (), s32[]{:S(2)}) async-start(), calls=%async_computation.2 | async-start | bytes 4194304 | tf_op jit(solution)/shard_map/psum | solution.py:27
  84.4 227.5 %all-reduce.7.cloned.1.call-start = ((), (), s32[]{:S(2)}) async-start(), calls=%async_computation.3 | async-start | bytes 4194304 | tf_op jit(solution)/shard_map/psum | solution.py:29
  154.2 806.1 %all-reduce.9.cloned.1.call-start = ((), (), s32[]{:S(2)}) async-start(), calls=%async_computation.4 | async-start | bytes 6291456 | tf_op jit(solution)/shard_map/psum | solution.py:32
  317.4 1.3 copy-start.6
  414.8 2.6 copy-start.11
  771.5 2.6 copy-start.2
  774.1 4.4 copy-start.7
  774.1 3.3 copy-start.13
  774.1 5.1 copy-start.4
  778.5 0.8 copy-start.9
  976.4 2.4 copy-start.8
  976.4 2.4 copy-start.10
  976.4 4.3 copy-start.5
  978.8 2.0 copy-start.12
  978.8 3.1 copy-start.1
Sparse Core Ops, SparseCore 0:
  10.6 70.3 reduce-scatter.1
  84.6 62.5 all-reduce.4
  154.3 157.5 all-reduce.6
  781.8 178.4 all-reduce.8
where the time goes:
time: 991 us
  waiting for transfers between devices  472 us (48%)
  other arithmetic  442 us (45%)
  matrix products  29.7 us (3%)
  local copies, waits for them, and re-layouts  17.8 us (2%)
  between operations  14 us (1%)
  blocking collectives  13.9 us (1%)
    another operation x9, other arithmetic, orthonormal(): factor = jnp.linalg.cholesky(gramian)  274 us
    psum x1, waiting for transfers between devices, on_device(): right_full = lax.psum(right_part, 'fsdp')  179 us
    another operation x4, other arithmetic, orthonormal(): lax.linalg.triangular_solve(factor, power, left_side=False, lower=True, t...  162 us
    psum x1, waiting for transfers between devices, on_device(): gramian = lax.psum(local_gram, 'fsdp')  157 us
    reduce_scatter x1, waiting for transfers between devices, on_device(): lax.psum_scatter(local_parts, 'rep', scatter_dimension=0, tiled=True)  73 us
    psum x1, waiting for transfers between devices, on_device(): power = lax.psum(partial_power, 'tp')  62.6 us
  transfers between devices with their start and end apart: 4, of which 4 were waited for; matrix products, arithmetic and copies ran while one was open for 0% of the time, Pallas kernels for 0%

commit v1 on v0

v1 whole, which is shorter than its diff:
```python
import jax
import jax.numpy as jnp
from jax import lax
from jax.experimental import pallas as pl
from jax.experimental.pallas import tpu as pltpu
from jax.sharding import PartitionSpec as P

D = 4096
FF = 1536
RANK = 256
NF = 16
BF = jnp.bfloat16
F32 = jnp.float32
HI = lax.Precision.HIGHEST
MESH = pl.DeviceIdType.MESH
VLIM = 50 * 1024 * 1024


def remote(src, dst, ssem, rsem, **dev):
    return pltpu.make_async_remote_copy(
        src_ref=src, dst_ref=dst, send_sem=ssem, recv_sem=rsem, device_id=dev, device_id_type=MESH
    )


def greet(peers):
    barrier = pltpu.get_barrier_semaphore()
    for dev in peers:
        pl.semaphore_signal(barrier, inc=1, device_id=dev, device_id_type=MESH)
    return barrier


def power_kernel(
    grad, mom, basis,
    buf_out, pow_out, gram_out,
    own, to_r, to_l, rel_a, rel_b, dir_a, dir_b, sum_a, sum_b,
    part, sib, cross, gsend, grecv, gsum, gall,
    load_sem, s_sem, r_sem, b_ssem, b_rsem, x_ssem, x_rsem, g_ssem, g_rsem, h_ssem, h_rsem,
):
    r = lax.axis_index("rep")
    f = lax.axis_index("fsdp")
    t = lax.axis_index("tp")
    xl, core = t // 2, t % 2
    right, left, across = (r + 1) % 4, (r + 3) % 4, (r + 2) % 4
    sibling = xl * 2 + (1 - core)
    partner = (1 - xl) * 2 + core

    loads = [
        pltpu.make_async_copy(grad.at[pl.ds(right * 8, 4)], to_r, load_sem.at[0]),
        pltpu.make_async_copy(grad.at[pl.ds(left * 8 + 4, 4)], to_l, load_sem.at[1]),
        pltpu.make_async_copy(grad.at[pl.ds(r * 8, 8)], own, load_sem.at[2]),
    ]
    for load in loads:
        load.start()

    barrier = greet([{"rep": right}, {"rep": left}, {"tp": sibling}, {"tp": partner}])

    def hello(d, c):
        pl.semaphore_signal(barrier, inc=1, device_id={"fsdp": (f + d) % NF}, device_id_type=MESH)
        return c

    lax.fori_loop(1, NF, hello, 0)
    pl.semaphore_wait(barrier, 4 + NF - 1)

    def relay(k):
        return [
            remote(grad.at[across * 8 + k], rel_a.at[k], s_sem.at[0, k], r_sem.at[0, k], rep=right),
            remote(grad.at[across * 8 + 4 + k], rel_b.at[k], s_sem.at[1, k], r_sem.at[1, k], rep=left),
        ]

    def direct(k):
        return [
            remote(grad.at[right * 8 + 4 + k], dir_b.at[k], s_sem.at[2, k], r_sem.at[2, k], rep=right),
            remote(grad.at[left * 8 + k], dir_a.at[k], s_sem.at[3, k], r_sem.at[3, k], rep=left),
        ]

    def summed(k):
        return [
            remote(to_r.at[k], sum_a.at[k], s_sem.at[4, k], r_sem.at[4, k], rep=right),
            remote(to_l.at[k], sum_b.at[k], s_sem.at[5, k], r_sem.at[5, k], rep=left),
        ]

    def start(copies):
        for copy in copies:
            copy.start()

    def forward(k):
        ra, rb = relay(k)
        sa, sb = summed(k)
        ra.wait_recv()
        to_r[k] = (to_r[k].astype(F32) + rel_a[k].astype(F32)).astype(BF)
        sa.start()
        rb.wait_recv()
        to_l[k] = (to_l[k].astype(F32) + rel_b[k].astype(F32)).astype(BF)
        sb.start()

    def to_sibling(k):
        return remote(part.at[k], sib.at[k // 2], b_ssem.at[k], b_rsem.at[k // 2], tp=sibling)

    def to_partner(k):
        return remote(part.at[k], cross, x_ssem, x_rsem, tp=partner)

    def expert(k, side):
        e = k + 4 * side
        s, d = (sum_a, dir_a) if side == 0 else (sum_b, dir_b)
        total = own[e].astype(F32) + s[k].astype(F32) + d[k].astype(F32)
        held = (mom[e].astype(F32) + total).astype(BF)
        buf_out[e] = held
        part[k, side] = jnp.dot(held, basis[e], preferred_element_type=F32)

    def finish(k):
        sa, sb = summed(k)
        db, da = direct(k)
        sa.wait_recv()
        da.wait_recv()
        expert(k, 0)
        sb.wait_recv()
        db.wait_recv()
        expert(k, 1)

        @pl.when(core != k % 2)
        def _():
            to_sibling(k).start()

    def combine(k):
        @pl.when(core == k % 2)
        def _():
            to_sibling(k).wait_recv()
            part[k] = part[k] + sib[k // 2]

            @pl.when(xl != k // 2)
            def _():
                to_partner(k).start()

    start(relay(0))
    start(relay(1))
    start(direct(0))
    loads[0].wait()
    loads[1].wait()
    forward(0)
    start(relay(2))
    start(direct(1))
    loads[2].wait()
    forward(1)
    start(relay(3))
    start(direct(2))
    finish(0)
    forward(2)
    combine(0)
    start(direct(3))
    finish(1)
    forward(3)
    combine(1)
    finish(2)
    combine(2)
    finish(3)
    combine(3)

    to_partner(0).wait_recv()
    for k in range(4):

        @pl.when(t == k)
        def _():
            pow_out[...] = part[k] + cross[...]

    for i in range(2):
        p = pow_out[i]
        g = lax.dot_general(p, p, (((0,), (0,)), ((), ())), precision=HI, preferred_element_type=F32)
        gsend[:, i] = g.reshape(NF, 16, RANK)
    grecv[f] = gsend[f]

    def scatter(d):
        to, frm = (f + d) % NF, (f + NF - d) % NF
        return (
            remote(gsend.at[to], grecv.at[f], g_ssem.at[d], g_rsem.at[d], fsdp=to),
            remote(gsend.at[to], grecv.at[frm], g_ssem.at[d], g_rsem.at[d], fsdp=to),
        )

    def gather(d):
        to, frm = (f + d) % NF, (f + NF - d) % NF
        return (
            remote(gsum, gall.at[f], h_ssem.at[d], h_rsem.at[d], fsdp=to),
            remote(gsum, gall.at[frm], h_ssem.at[d], h_rsem.at[d], fsdp=to),
        )

    def each(body):
        def step(d, c):
            body(d)
            return c

        lax.fori_loop(1, NF, step, 0)

    each(lambda d: scatter(d)[0].start())
    each(lambda d: scatter(d)[1].wait_recv())
    gsum[...] = jnp.sum(grecv[...], axis=0)
    each(lambda d: gather(d)[0].start())
    gall[f] = gsum[...]
    each(lambda d: gather(d)[1].wait_recv())
    for i in range(2):
        gram_out[i] = gall[:, i].reshape(RANK, RANK)

    each(lambda d: scatter(d)[0].wait_send())
    each(lambda d: gather(d)[0].wait_send())
    for k in range(4):
        for copy in relay(k) + direct(k) + summed(k):
            copy.wait_send()

        @pl.when(core != k % 2)
        def _():
            to_sibling(k).wait_send()

        @pl.when((core == k % 2) & (xl != k // 2))
        def _():
            to_partner(k).wait_send()


def power_call(grad, momentum, basis):
    chunk = (4, 256, 384)
    sem = pltpu.SemaphoreType.DMA
    vm = pl.BlockSpec(memory_space=pltpu.VMEM)
    return pl.pallas_call(
        power_kernel,
        out_shape=(
            jax.ShapeDtypeStruct((8, 256, 384), BF),
            jax.ShapeDtypeStruct((2, RANK, RANK), F32),
            jax.ShapeDtypeStruct((2, RANK, RANK), F32),
        ),
        in_specs=[pl.BlockSpec(memory_space=pl.ANY), vm, vm],
        out_specs=(vm, vm, vm),
        scratch_shapes=[pltpu.VMEM((8, 256, 384), BF)]
        + [pltpu.VMEM(chunk, BF)] * 8
        + [
            pltpu.VMEM((4, 2, 256, 256), F32),
            pltpu.VMEM((2, 2, 256, 256), F32),
            pltpu.VMEM((2, 256, 256), F32),
            pltpu.VMEM((NF, 2, 16, 256), F32),
            pltpu.VMEM((NF, 2, 16, 256), F32),
            pltpu.VMEM((2, 16, 256), F32),
            pltpu.VMEM((NF, 2, 16, 256), F32),
            sem((3,)), sem((6, 4)), sem((6, 4)), sem((4,)), sem((2,)), sem, sem,
            sem((NF,)), sem((NF,)), sem((NF,)), sem((NF,)),
        ],
        compiler_params=pltpu.CompilerParams(
            collective_id=0, has_side_effects=True, vmem_limit_bytes=VLIM
        ),
        name="power",
    )(grad, momentum, basis)


NB = 64


def factor_kernel(gram, power, ortho, work):
    def iota(shape, axis):
        return lax.broadcasted_iota(jnp.int32, shape, axis)

    eye = (iota((RANK, RANK), 0) == iota((RANK, RANK), 1)).astype(F32)
    small = (iota((NB, NB), 0) == iota((NB, NB), 1)).astype(F32)
    sub = iota((8, 128), 0)
    for i in range(2):
        work[i, :, :RANK] = gram[i]
        work[i, :, RANK:] = eye
    for b in range(RANK // NB):
        lo, hi = NB * b, NB * (b + 1)
        rows = []
        for i in range(2):
            m = jnp.concatenate([work[i, lo:hi, lo:hi], small], axis=1)
            rows.append([m[8 * q : 8 * q + 8] for q in range(NB // 8)])
        for q0 in range(NB // 8):
            diag = [None, None]
            for jj in range(8):
                j = 8 * q0 + jj
                for i in range(2):
                    m = rows[i]
                    cols = [jnp.broadcast_to(m[q][:, j : j + 1], (8, 128)) for q in range(q0, NB // 8)]
                    scaled = m[q0][jj : jj + 1] / cols[0][jj : jj + 1]
                    diag[i] = cols[0] if jj == 0 else jnp.where(sub == jj, cols[0], diag[i])
                    m[q0] = m[q0] - jnp.where(sub > jj, cols[0], 0.0) * scaled
                    for q in range(q0 + 1, NB // 8):
                        m[q] = m[q] - cols[q - q0] * scaled
            for i in range(2):
                rows[i][q0] = rows[i][q0] * lax.rsqrt(diag[i])
        for i in range(2):
            inv = jnp.concatenate(rows[i], axis=0)[:, NB:]
            a, z = hi // 128 * 128, -(-(RANK + hi) // 128) * 128
            x = jnp.dot(inv, work[i, lo:hi, a:z], precision=HI, preferred_element_type=F32)
            work[i, lo:hi, a:z] = x
            if hi < RANK:
                panel = x[:, hi - a : RANK - a]
                work[i, hi:, a:z] = work[i, hi:, a:z] - lax.dot_general(
                    panel, x, (((0,), (0,)), ((), ())), precision=HI, preferred_element_type=F32
                )
    for i in range(2):
        ortho[i] = lax.dot_general(
            power[i], work[i, :, RANK:], (((1,), (1,)), ((), ())), precision=HI, preferred_element_type=F32
        ).astype(BF)


def factor_call(gram, power):
    vm = pl.BlockSpec(memory_space=pltpu.VMEM)
    return pl.pallas_call(
        factor_kernel,
        out_shape=jax.ShapeDtypeStruct((2, 256, RANK), BF),
        in_specs=[vm, vm],
        out_specs=vm,
        scratch_shapes=[pltpu.VMEM((2, RANK, 2 * RANK), F32)],
        compiler_params=pltpu.CompilerParams(vmem_limit_bytes=VLIM),
        name="factor",
    )(gram, power)


def right_kernel(
    ortho, buf,
    ortho_all, right_all, squares,
    acc, flow, swap_to, swap_from, sq_mine, sq_recv,
    o_ssem, o_rsem, f_ssem, f_rsem, w_ssem, w_rsem, a_ssem, a_rsem, q_ssem, q_rsem,
):
    f = lax.axis_index("fsdp")
    t = lax.axis_index("tp")
    xl, core = t // 2, t % 2
    sibling = xl * 2 + (1 - core)
    partner = (1 - xl) * 2 + core
    diagonal = (1 - xl) * 2 + (1 - core)
    z, xh = f // 2, f % 2
    up, down = ((z + 1) % 8) * 2 + xh, ((z + 7) % 8) * 2 + xh
    other = z * 2 + (1 - xh)

    barrier = greet(
        [{"tp": sibling}, {"tp": partner}, {"tp": diagonal}, {"fsdp": up}, {"fsdp": down}, {"fsdp": other}]
    )
    ortho_all[t] = ortho[...]
    pl.semaphore_wait(barrier, 6)

    near = remote(ortho_all.at[t], ortho_all.at[t], o_ssem.at[0], o_rsem.at[0], tp=sibling)
    far = remote(ortho_all.at[t], ortho_all.at[t], o_ssem.at[1], o_rsem.at[1], tp=partner)
    passed = remote(ortho_all.at[partner], ortho_all.at[partner], o_ssem.at[2], o_rsem.at[2], tp=sibling)
    near_in = remote(ortho_all.at[sibling], ortho_all.at[sibling], o_ssem.at[0], o_rsem.at[0], tp=sibling)
    far_in = remote(ortho_all.at[partner], ortho_all.at[partner], o_ssem.at[1], o_rsem.at[1], tp=partner)
    passed_in = remote(ortho_all.at[diagonal], ortho_all.at[diagonal], o_ssem.at[2], o_rsem.at[2], tp=sibling)
    far.start()
    near.start()

    def product(owner):
        for side in range(2):
            acc[owner + 4 * side] = lax.dot_general(
                buf[owner + 4 * side], ortho_all[owner, side],
                (((0,), (0,)), ((), ())), preferred_element_type=F32,
            ).astype(BF)

    product(t)
    near_in.wait_recv()
    product(sibling)
    far_in.wait_recv()
    passed.start()
    product(partner)
    passed_in.wait_recv()
    product(diagonal)

    def half(ref, at, h):
        return ref.at[at, pl.ds(192 * h, 192)]

    def hop(way, left, h):
        target = (z + left) % 8 if way == 0 else (z + 8 - left) % 8
        return remote(
            half(acc, target, h), flow.at[way, left - 1, h],
            f_ssem.at[way, left - 1, h], f_rsem.at[way, left - 1, h],
            fsdp=up if way == 0 else down,
        )

    def long(way):
        return way

    hop(0, 4, long(0)).start()
    hop(1, 4, long(1)).start()
    hop(0, 3, 1 - long(0)).start()
    hop(1, 3, 1 - long(1)).start()
    for left in (4, 3, 2):
        for way in range(2):
            halves = (long(way),) if left == 4 else (long(way), 1 - long(way))
            for h in halves:
                hop(way, left, h).wait_recv()
                target = (z + left - 1) % 8 if way == 0 else (z + 9 - left) % 8
                at = pl.ds(192 * h, 192)
                acc[target, at] = (
                    acc[target, at].astype(F32) + flow[way, left - 1, h].astype(F32)
                ).astype(BF)
                hop(way, left - 1, h).start()
    swap = remote(swap_to, swap_from, w_ssem, w_rsem, fsdp=other)
    for h in range(2):
        for way in range(2):
            hop(way, 1, h).wait_recv()
        at = pl.ds(192 * h, 192)
        swap_to[at] = (
            acc[z, at].astype(F32) + flow[0, 0, h].astype(F32) + flow[1, 0, h].astype(F32)
        ).astype(BF)
    swap.start()
    swap.wait_recv()
    right_all[z] = (swap_to[...].astype(F32) + swap_from[...].astype(F32)).astype(BF)

    def spread(way, gone, h):
        source = (z + 8 - gone) % 8 if way == 0 else (z + gone) % 8
        return remote(
            half(right_all, source, h), half(right_all, source, h),
            a_ssem.at[way, gone, h], a_rsem.at[way, gone, h],
            fsdp=up if way == 0 else down,
        )

    def arrived(way, gone, h):
        source = (z + 7 - gone) % 8 if way == 0 else (z + gone + 1) % 8
        return remote(
            half(right_all, source, h), half(right_all, source, h),
            a_ssem.at[way, gone, h], a_rsem.at[way, gone, h],
            fsdp=up if way == 0 else down,
        )

    for h in range(2):
        for way in range(2):
            spread(way, 0, h).start()
    for gone in range(4):
        for way in range(2):
            halves = (long(way), 1 - long(way)) if gone < 3 else (long(way),)
            for h in halves:
                arrived(way, gone, h).wait_recv()
                if gone + 1 < (4 if h == long(way) else 3):
                    spread(way, gone + 1, h).start()

    for e in range(8):
        full = right_all[e].astype(F32)
        sq_mine[e : e + 1] = jnp.sum(full * full, axis=0, keepdims=True)

    def tell(n, dev):
        return remote(sq_mine, sq_recv.at[n], q_ssem.at[n], q_rsem.at[n], tp=dev)

    tells = [tell(0, sibling), tell(1, partner), tell(2, diagonal)]
    for copy in tells:
        copy.start()
    for copy in tells:
        copy.wait_recv()
    squares[...] = (sq_mine[...] + sq_recv[0]) + (sq_recv[1] + sq_recv[2])

    near.wait_send()
    far.wait_send()
    passed.wait_send()
    swap.wait_send()
    for copy in tells:
        copy.wait_send()
    for way in range(2):
        for h in range(2):
            for n in range(4 if h == long(way) else 3):
                hop(way, n + 1, h).wait_send()
                spread(way, n, h).wait_send()


def right_call(ortho, buf):
    sem = pltpu.SemaphoreType.DMA
    vm = pl.BlockSpec(memory_space=pltpu.VMEM)
    return pl.pallas_call(
        right_kernel,
        out_shape=(
            jax.ShapeDtypeStruct((4, 2, 256, RANK), BF),
            jax.ShapeDtypeStruct((8, 384, RANK), BF),
            jax.ShapeDtypeStruct((8, RANK), F32),
        ),
        in_specs=[vm, vm],
        out_specs=(vm, vm, vm),
        scratch_shapes=[
            pltpu.VMEM((8, 384, RANK), BF),
            pltpu.VMEM((2, 4, 2, 192, RANK), BF),
            pltpu.VMEM((384, RANK), BF),
            pltpu.VMEM((384, RANK), BF),
            pltpu.VMEM((8, RANK), F32),
            pltpu.VMEM((3, 8, RANK), F32),
            sem((3,)), sem((3,)), sem((2, 4, 2)), sem((2, 4, 2)), sem, sem,
            sem((2, 4, 2)), sem((2, 4, 2)), sem((3,)), sem((3,)),
        ],
        compiler_params=pltpu.CompilerParams(
            collective_id=1, has_side_effects=True, vmem_limit_bytes=VLIM
        ),
        name="right",
    )(ortho, buf)


def output_kernel(buf, ortho, right, squares, mom_next, basis_next, update):
    e = pl.program_id(0)
    r = right[0]
    scale = lax.rsqrt(squares[pl.ds(e, 1)] + 1e-06)
    nxt = (r.astype(F32) * scale).astype(BF)
    basis_next[0] = nxt
    o = ortho[0, 0]
    dims = (((1,), (1,)), ((), ()))
    back = lax.dot_general(o, r, dims, preferred_element_type=F32)
    mom_next[0] = (buf[0].astype(F32) - 0.05 * back).astype(BF)
    up = lax.dot_general(o, nxt, dims, preferred_element_type=F32)
    update[0] = ((D * FF / RANK) ** 0.5 * up).astype(BF)


def output_call(buf, ortho, right, squares):
    wide = pl.BlockSpec((1, 256, 384), lambda e: (e, 0, 0))
    tall = pl.BlockSpec((1, 384, RANK), lambda e: (e, 0, 0))
    return pl.pallas_call(
        output_kernel,
        grid=(8,),
        out_shape=(
            jax.ShapeDtypeStruct((8, 256, 384), BF),
            jax.ShapeDtypeStruct((8, 384, RANK), BF),
            jax.ShapeDtypeStruct((8, 256, 384), BF),
        ),
        in_specs=[
            wide,
            pl.BlockSpec((1, 1, 256, RANK), lambda e: (e % 4, e // 4, 0, 0)),
            tall,
            pl.BlockSpec((8, RANK), lambda e: (0, 0)),
        ],
        out_specs=(wide, tall, wide),
        compiler_params=pltpu.CompilerParams(vmem_limit_bytes=VLIM),
        name="outputs",
    )(buf, ortho, right, squares)


def on_device(grad_parts, momentum, basis):
    buf, power, gram = power_call(grad_parts[0], momentum, basis)
    ortho = factor_call(gram, power)
    ortho_all, right, squares = right_call(ortho, buf)
    return output_call(buf, ortho_all, right, squares)


def solution(mesh):
    placed = (P("rep", None, "fsdp", "tp"), P("rep", "fsdp", "tp"), P("rep", "tp", None))
    return jax.shard_map(
        on_device,
        mesh=mesh,
        in_specs=placed,
        out_specs=(P("rep", "fsdp", "tp"), P("rep", "tp", None), P("rep", "fsdp", "tp")),
        check_vma=False,
    )
```

time: 991 us -> 202 us (0.20)
  waiting for transfers between devices: 472 us -> 0 us
  other arithmetic: 442 us -> 0 us
  Pallas kernels: 0 us -> 199 us
  matrix products: 29.7 us -> 0 us
  local copies, waits for them, and re-layouts: 17.8 us -> 2.3 us
  blocking collectives: 13.9 us -> 0 us
  between operations: 14 us -> 0.67 us
    another operation x13 -> x0, other arithmetic: 436 us -> none  [the longest x9 274 us: orthonormal(): factor = jnp.linalg.cholesky(gramian)]
    psum x3 -> x0, waiting for transfers between devices: 399 us -> none  [the longest x1 179 us: on_device(): right_full = lax.psum(right_part, 'fsdp')]
    pallas_call x0 -> x4, Pallas kernels: none -> 199 us  [the longest x1 98.7 us: power_call(): pl.pallas_call(power_kernel, out_shape=(jax.ShapeDtypeStruct((8, 256, 384...]
    reduce_scatter x1 -> x0, waiting for transfers between devices: 73 us -> none  [on_device(): lax.psum_scatter(local_parts, 'rep', scatter_dimension=0, tiled=True)]
    dot_general x5 -> x0, matrix products: 17.1 us -> none  [the longest x1 7.03 us: on_device(): jnp.einsum('emr,ems->ers', power, power, precision=lax.Precision.HIGHEST)]
    psum x1 -> x0, blocking collectives: 13.9 us -> none  [on_device(): squares = lax.psum(jnp.sum(right_full * right_full, axis=1), 'tp')]
    another operation x5 -> x0, matrix products: 12.6 us -> none  [the longest x3 6.89 us: orthonormal(): lax.linalg.triangular_solve(factor, power, left_side=False, lower=True, t...]
    another operation x9 -> x0, local copies, waits for them, and re-layouts: 11.6 us -> none
  transfers between devices with their start and end apart: 4 -> 0, of which waited for: 4 -> 0; matrix products, arithmetic and copies ran while one was open for 0% -> 0% of each run, Pallas kernels for 0% -> 0%
where the time goes in v1:
time: 202 us
  Pallas kernels  199 us (99%)
  local copies, waits for them, and re-layouts  2.3 us (1%)
    pallas_call x1, Pallas kernels, power_call(): pl.pallas_call(power_kernel, out_shape=(jax.ShapeDtypeStruct((8, 256, 384...  98.7 us
    pallas_call x1, Pallas kernels, right_call(): pl.pallas_call(right_kernel, out_shape=(jax.ShapeDtypeStruct((4, 2, 256,...  67.7 us
    pallas_call x1, Pallas kernels, factor_call(): pl.pallas_call(factor_kernel, out_shape=jax.ShapeDtypeStruct((2, 256, RAN...  25.6 us
    pallas_call x1, Pallas kernels, output_call(): pl.pallas_call(output_kernel, grid=(8,), out_shape=(jax.ShapeDtypeStruct(...  6.7 us

profile of v1, /device:TPU:1, one launch (start us, length us, event | category | flops | bytes accessed | tf_op | source)
XLA Modules:
  0.0 201.6 jit_solution(1897278044789243835)
XLA Ops:
  0.6 98.7 %power.1 = (bf16[8,256,384]{2,1,0:T(8,128)(2,1)S(1)}, f32[2,256,256]{2,1,0:T(8,128)S(1)}, f32[2,256,256]{2,1,0:T(8,128)S(1)}) custom-call(bf16[32,256,384]{2,1,0:T(8,128)(2,1)} %bitcast.1, bf16[8,256,384]{2,1,0:T(8,128)(2,1)} %mom.1, bf16[8,384,256]{2,1,0:T(8,128)(2,1)} %basis.1), custom_call_target="tpu_custom_call" | custom-call | tf_op jit(solution)/shard_map/power/pallas_call | solution.py:220
  99.3 0.0 copy-start
  99.3 1.1 copy-done
  100.5 0.0 copy-start.1
  100.5 25.6 %factor.1.ortho = bf16[2,256,256]{2,1,0:T(8,128)(2,1)S(1)} custom-call(f32[2,256,256]{2,1,0:T(8,128)S(1)} %get-tuple-element.10.gram, f32[2,256,256]{2,1,0:T(8,128)S(1)} %get-tuple-element.11.power), custom_call_target="tpu_custom_call" | custom-call | tf_op jit(solution)/shard_map/factor/pallas_call | solution.py:300
  126.1 67.7 %right.1 = (bf16[4,2,256,256]{3,2,1,0:T(8,128)(2,1)S(1)}, bf16[8,384,256]{2,1,0:T(8,128)(2,1)S(1)}, f32[8,256]{1,0:T(8,128)S(1)}) custom-call(bf16[2,256,256]{2,1,0:T(8,128)(2,1)S(1)} %factor.1.ortho, bf16[8,256,384]{2,1,0:T(8,128)(2,1)} %copy-done), custom_call_target="tpu_custom_call" | custom-call | tf_op jit(solution)/shard_map/right/pallas_call | solution.py:456
  193.8 0.0 copy-start.2
  193.8 1.2 copy-done.2
  194.9 0.0 copy-done.1
  194.9 6.7 %outputs.1 = (bf16[8,256,384]{2,1,0:T(8,128)(2,1)}, bf16[8,384,256]{2,1,0:T(8,128)(2,1)}, bf16[8,256,384]{2,1,0:T(8,128)(2,1)}) custom-call(bf16[8,256,384]{2,1,0:T(8,128)(2,1)S(1)} %copy-done.1, bf16[4,2,256,256]{3,2,1,0:T(8,128)(2,1)S(1)} %get-tuple-element.12.ortho, bf16[8,384,256]{2,1,0:T(8,128)(2,1)} %copy-done.2, f32[8,256]{1,0:T(8,128)S(1)} %get-tuple-element.14.squares), custom_call_target="tpu_custom_call" | custom-call | tf_op jit(solution)/shard_map/outputs/pallas_call | solution.py:499
Async XLA Ops:
  99.3 1.1 copy-start
  100.5 94.5 %copy-start.1 = (bf16[8,256,384]{2,1,0:T(8,128)(2,1)S(1)}, bf16[8,256,384]{2,1,0:T(8,128)(2,1)}, u32[]{:S(2)}) copy-start(bf16[8,256,384]{2,1,0:T(8,128)(2,1)} %copy-done) | copy-start | bytes 4718596
  193.8 1.2 copy-start.2
